TPU v7x, 32 devices: a whole 2x2x4 slice. The times are simulated.
32 devices in a mesh: head: 2 (over x), ctx: 16 (over z, y, core).
Axes of the slice: x: 2, y: 2, z: 4, core: 2. Of those that a mesh axis runs over, the one named last changes fastest.
Arguments:
- queries: bfloat16 [16384, 2048], P('ctx', 'head'), may hold values from -6 to 6
- key_vectors: bfloat16 [16384, 2048], P('ctx', 'head'), may hold values from -6 to 6
- value_vectors: bfloat16 [16384, 2048], P('ctx', 'head'), may hold values from -6 to 6
- out_grad: bfloat16 [16384, 2048], P('ctx', 'head'), may hold values from -6 to 6
- segment_ids: int32 [16384], P('ctx'), may hold values from 0 to 7, never falling along the last dimension, each value on 1 to 4096 neighbouring positions
- head_gain: float32 [16], P('head'), may hold values from 0.3 to 3
Outputs:
- attended: bfloat16 [16384, 2048], P('ctx', 'head')
- grad_queries: bfloat16 [16384, 2048], P('ctx', 'head')
- grad_keys: bfloat16 [16384, 2048], P('ctx', 'head')
- grad_values: bfloat16 [16384, 2048], P('ctx', 'head')
Inputs may be any that keep to these rules, and one draw needn't show every extreme that they name: `segment_ids`: document numbers never fall along the sequence; every document covers 1 to 4096 positions and one covers exactly 4096.
All inputs are finite; a program needn't handle non-finite values.
Results may differ from a plain program's by a relative error of at most 0.0058.
Values sent between devices are 32-bit elements; how exact they have to be, the bound alone decides.
A program may use at most 128 MiB of HBM per device.

v0:
```python
import jax
import jax.numpy as jnp
from jax import lax
from jax.sharding import PartitionSpec as P

HEADS = 16
HS = 128


EPS = 1e-05


def entering(value, axis, combine, identity, reverse):
    size, index = (lax.axis_size(axis), lax.axis_index(axis))
    everything = jax.tree.map(lambda part: lax.all_gather(part, axis), value)
    start = jax.tree.map(
        lambda part, zero: jnp.broadcast_to(jnp.asarray(zero, part.dtype), part.shape),
        value,
        identity,
    )

    def turn(k, before):
        at = size - 1 - k if reverse else k
        reached = at > index if reverse else at < index
        new = combine(before, jax.tree.map(lambda part: part[at], everything))
        return jax.tree.map(lambda a, b: jnp.where(reached, a, b), new, before)

    return lax.fori_loop(0, size, turn, start)


def join_forward(earlier, later):
    earlier_none = earlier[0] < 0.0
    later_none = later[0] < 0.0
    joined = (earlier[1] == later[0]) & (later[0] == later[1])
    state = jnp.where(later_none, earlier[2], jnp.where(joined, earlier[2] + later[2], later[2]))
    opening = jnp.where(earlier_none, later[0], earlier[0])
    closing = jnp.where(later_none, earlier[1], later[1])
    return (opening, closing, state)


def join_backward(earlier, later):
    earlier_none = earlier[0] < 0.0
    later_none = later[0] < 0.0
    joined = (later[1] == earlier[0]) & (later[0] == later[1])
    state = jnp.where(later_none, earlier[2], jnp.where(joined, earlier[2] + later[2], later[2]))
    opening = jnp.where(later_none, earlier[0], later[0])
    closing = jnp.where(earlier_none, later[1], earlier[1])
    return (opening, closing, state)


def per_device(queries, key_vectors, value_vectors, out_grad, segment_ids, head_gain):
    row_count = queries.shape[0]
    local_heads = head_gain.shape[0]
    width = HEADS * HS
    layout = (row_count, local_heads, HS)
    query_rows = queries.reshape(layout)
    key_rows = key_vectors.reshape(layout)
    value_rows = value_vectors.reshape(layout)
    opening_id = segment_ids[0]
    closing_id = segment_ids[-1]
    position = jnp.arange(row_count)
    allowed = (
        (position[:, None] >= position[None, :]) & (segment_ids[:, None] == segment_ids[None, :])
    )[None]
    at_open = (segment_ids == opening_id)[:, None, None]
    at_close = (segment_ids == closing_id)[:, None, None]
    zero_half = jnp.zeros((), jnp.bfloat16)
    scores = jnp.einsum("thd,shd->hts", query_rows, key_rows, preferred_element_type=jnp.float32)
    probs = jnp.where(allowed, scores, 0.0).astype(jnp.bfloat16)
    local_out = jnp.einsum("hts,shd->thd", probs, value_rows, preferred_element_type=jnp.float32)
    tail = jnp.einsum(
        "shd,she->hde",
        jnp.where(at_close, key_rows, zero_half),
        value_rows,
        preferred_element_type=jnp.float32,
    )
    open_mark = opening_id.astype(jnp.float32)
    close_mark = closing_id.astype(jnp.float32)
    blank = jnp.zeros_like(tail)
    no_mark = jnp.float32(-1.0)
    prior = entering(
        (open_mark, close_mark, tail), "ctx", join_forward, (no_mark, no_mark, blank), False
    )
    incoming = jnp.where(prior[1] == open_mark, prior[2], 0.0)
    state_in = incoming.astype(jnp.bfloat16)
    carried = jnp.einsum("thd,hde->the", query_rows, state_in, preferred_element_type=jnp.float32)
    attn = local_out + jnp.where(at_open, carried, 0.0)
    gain = head_gain[None, :, None]
    scaled = attn * gain
    grad_rows = out_grad.reshape(layout).astype(jnp.float32)
    power, cross = lax.psum(
        (jnp.sum(scaled * scaled, axis=(1, 2)), jnp.sum(grad_rows * scaled, axis=(1, 2))), "head"
    )
    scale = lax.rsqrt(power / width + EPS)[:, None, None]
    cross = cross[:, None, None]
    attended = (scaled * scale).astype(jnp.bfloat16)
    inner = (gain * (grad_rows * scale - scaled * cross * scale * scale * scale / width)).astype(
        jnp.bfloat16
    )
    dscores = jnp.einsum("the,she->hts", inner, value_rows, preferred_element_type=jnp.float32)
    dprobs = jnp.where(allowed, dscores, 0.0).astype(jnp.bfloat16)
    grad_q = jnp.einsum("hts,shd->thd", dprobs, key_rows, preferred_element_type=jnp.float32)
    grad_q = grad_q + jnp.where(
        at_open,
        jnp.einsum("the,hde->thd", inner, state_in, preferred_element_type=jnp.float32),
        0.0,
    )
    back_tail = jnp.einsum(
        "thd,the->hde",
        jnp.where(at_open, query_rows, zero_half),
        inner,
        preferred_element_type=jnp.float32,
    )
    after = entering(
        (open_mark, close_mark, back_tail), "ctx", join_backward, (no_mark, no_mark, blank), True
    )
    returning = jnp.where(after[0] == close_mark, after[2], 0.0)
    state_grad = returning.astype(jnp.bfloat16)
    grad_k = jnp.einsum("hts,thd->shd", dprobs, query_rows, preferred_element_type=jnp.float32)
    grad_k = grad_k + jnp.where(
        at_close,
        jnp.einsum("hde,she->shd", state_grad, value_rows, preferred_element_type=jnp.float32),
        0.0,
    )
    grad_v = jnp.einsum("hts,the->she", probs, inner, preferred_element_type=jnp.float32)
    grad_v = grad_v + jnp.where(
        at_close,
        jnp.einsum("hde,shd->she", state_grad, key_rows, preferred_element_type=jnp.float32),
        0.0,
    )
    flat = (row_count, local_heads * HS)
    return (
        attended.reshape(flat),
        grad_q.astype(jnp.bfloat16).reshape(flat),
        grad_k.astype(jnp.bfloat16).reshape(flat),
        grad_v.astype(jnp.bfloat16).reshape(flat),
    )


def solution(mesh):
    in_specs = (
        P("ctx", "head"),
        P("ctx", "head"),
        P("ctx", "head"),
        P("ctx", "head"),
        P("ctx"),
        P("head"),
    )
    out_specs = (P("ctx", "head"), P("ctx", "head"), P("ctx", "head"), P("ctx", "head"))
    return jax.shard_map(
        per_device, mesh=mesh, in_specs=in_specs, out_specs=out_specs, check_vma=False
    )
```

profile of v0, /device:TPU:0, one launch (start us, length us, event | category | flops | bytes accessed | tf_op | source)
XLA Modules:
  0.0 412.8 jit_solution(11004657943211261623)
XLA Ops:
  7.2 1.4 fusion.32
  8.7 3.5 copy.62
  12.2 4.1 copy.35
  16.3 1.3 broadcast_compare_fusion
  17.6 3.2 fusion.9
  24.3 35.5 %all-reduce.2 = (f32[16]{0:T(128)S(1)}, f32[16]{0:T(128)S(1)}) all-reduce(f32[16]{0:T(128)S(1)} %dynamic-update-slice, f32[16]{0:T(128)S(1)} %dynamic-update-slice.1), channel_id=1, replica_groups=mesh['head'=2,'ctx'=16] {'ctx'}, use_global_device_ids=true, to_apply=%add | all-reduce | flops 32 | bytes 256
  59.8 3.9 copy.59
  63.7 4.1 %copy.39 = f32[1024,1024]{0,1:T(8,128)} copy(bf16[1024,1024]{1,0:T(8,128)(2,1)} %param.13) | data formatting | bytes 6291456 | tf_op jit(solution)/shard_map/convert_element_type | solution.py:90
  68.5 10.9 %select_convert_fusion.1 = bf16[8,1024,1024]{2,1,0:T(8,128)(2,1)} fusion(pred[1024,1024]{1,0:T(8,128)(4,1)S(1)} %fusion.3, bf16[1024,8,128]{0,2,1:T(8,128)(2,1)} %bitcast.103, bf16[1024,1024]{1,0:T(8,128)(2,1)} %param.11), kind=kOutput, calls=%fused_computation.5 | convolution fusion | flops 2164260864 | bytes 22020096 | tf_op jit(solution)/shard_map/thd,shd->hts/dot_general | solution.py:68
  79.4 11.1 %fusion.4 = f32[8,1024,128]{1,2,0:T(8,128)} fusion(bf16[8,1024,1024]{2,1,0:T(8,128)(2,1)} %select_convert_fusion.1, bf16[1024,1024]{1,0:T(8,128)(2,1)S(1)} %copy-done), kind=kOutput, calls=%fused_computation.19 | convolution fusion | flops 2147483648 | bytes 23068672 | tf_op jit(solution)/shard_map/hts,shd->thd/dot_general | solution.py:70
  90.5 8.4 %all-gather.5.cloned.1.call-done = f32[128,128,128]{2,1,0:T(8,128)} async-done(((f32[8,128,128]{2,1,0:T(8,128)}), f32[128,128,128]{2,1,0:T(8,128)}) %all-gather.5.cloned.1.call-update) | async-done | bytes 8388624 | tf_op jit(solution)/shard_map/all_gather | solution.py:15
  98.8 94.4 %while.34 = (s32[]{:T(128)}, f32[]{:T(128)}, f32[8,128,128]{2,1,0:T(8,128)S(1)}, s32[]{:T(128)}, f32[16]{0:T(128)S(1)}, /*index=5*/f32[16]{0:T(128)S(1)}, f32[16...) while((s32[]{:T(128)}, f32[]{:T(128)}, f32[8,128,128]{2,1,0:T(8,128)S(1)}, s32[]{:T(128)}, ...), condition=%wide.region_1.2_spmd.clone, body=%wide.region_0.1_spmd.clone.sunk | while | flops 655370 | bytes 1573071 | solution.py:28
  102.7 1.3 select_select_fusion.4
  108.6 1.3 select_select_fusion.4
  193.3 7.5 %multiply_reduce_fusion = (f32[1024]{0:T(1024)S(1)}, f32[1024]{0:T(1024)S(1)}, f32[1024,8,128]{0,2,1:T(8,128)}) fusion(f32[1024,1024]{0,1:T(8,128)} %copy.39, f32[8]{0:T(128)S(1)} %copy-done.9, bf16[1024,8,128]{0,2,1:T(8,128)(2,1)} %bitcast.104, f32[8,128,128]{2,1,0:T(8,128)S(1)} %get-tuple-element.307, pred[]{:T(512)S(6)} %eq.76, ...), kind=kOutput, calls=%fused_computation.14 | convolution fusion | flops 275904512 | bytes 15213601 | tf_op jit(solution)/shard_map/thd,hde->the/dot_general | solution.py:86
  200.7 5.0 %all-reduce.3 = (f32[1024]{0:T(1024)S(1)}, f32[1024]{0:T(1024)S(1)}) all-reduce(f32[1024]{0:T(1024)S(1)} %get-tuple-element.367, f32[1024]{0:T(1024)S(1)} %get-tuple-element.366), channel_id=1, replica_groups=mesh['head'=2,'ctx'=16] {'head'}, use_global_device_ids=true, to_apply=%region_3.4 | all-reduce | flops 2048 | bytes 16384 | tf_op jit(solution)/shard_map/psum | solution.py:91
  205.7 6.4 %multiply_convert_fusion = (bf16[1024,8,128]{0,2,1:T(8,128)(2,1)S(1)}, bf16[1024,8,128]{0,2,1:T(8,128)(2,1)}) fusion(f32[1024,8,128]{0,2,1:T(8,128)} %get-tuple-element.406, f32[1024,8,128]{0,2,1:T(8,128)} %bitcast.102, f32[1024]{0:T(1024)S(1)} %get-tuple-element.399, f32[1024]{0:T(1024)S(1)} %add_rsqrt_fusion, f32[8]{0:T(128)S(1)} %copy-done.9), kind=kLoop, calls=%fused_computation.13 | loop fusion | flops 11534336 | bytes 12591136 | tf_op jit(solution)/shard_map/convert_element_type | solution.py:97
  212.1 1.4 copy-done.2
  213.4 1.5 fusion.13
  215.0 10.6 %select_convert_fusion = bf16[8,1024,1024]{2,1,0:T(8,128)(2,1)} fusion(pred[1024,1024]{1,0:T(8,128)(4,1)} %copy-done.7, bf16[1024,8,128]{0,2,1:T(8,128)(2,1)} %copy-done.2, bf16[1024,1024]{1,0:T(8,128)(2,1)S(1)} %copy-done), kind=kOutput, calls=%fused_computation.4 | convolution fusion | flops 2164260864 | bytes 22020096 | tf_op jit(solution)/shard_map/the,she->hts/dot_general | solution.py:100
  225.5 9.4 %fusion.33 = f32[8,1024,128]{1,2,0:T(8,128)S(1)} fusion(bf16[8,1024,1024]{2,1,0:T(8,128)(2,1)} %select_convert_fusion, bf16[1024,8,128]{0,2,1:T(8,128)(2,1)S(1)} %copy-done.5), kind=kOutput, calls=%fused_computation.53 | convolution fusion | flops 2147483648 | bytes 23068672 | tf_op jit(solution)/shard_map/hts,shd->thd/dot_general | solution.py:102
  235.0 2.0 fusion.1
  237.0 3.9 copy.51
  240.9 3.9 copy.50
  244.9 11.8 %fusion.34 = f32[8,128,1024]{2,1,0:T(8,128)} fusion(bf16[1024,8,128]{0,2,1:T(8,128)(2,1)} %copy-done.2, bf16[8,1024,1024]{2,1,0:T(8,128)(2,1)} %select_convert_fusion.1), kind=kOutput, calls=%fused_computation.54 | convolution fusion | flops 2147483648 | bytes 23068672 | tf_op jit(solution)/shard_map/hts,the->she/dot_general | solution.py:125
  256.6 31.6 %all-gather.7.cloned.1.call-done = f32[128,128,128]{2,1,0:T(8,128)} async-done(((f32[8,128,128]{2,1,0:T(8,128)}), f32[128,128,128]{2,1,0:T(8,128)}) %all-gather.7.cloned.1.call-update) | async-done | bytes 8388624 | tf_op jit(solution)/shard_map/all_gather | solution.py:15
  288.3 91.9 %while.35 = (s32[]{:T(128)}, f32[]{:T(128)}, f32[8,128,128]{2,1,0:T(8,128)S(1)}, s32[]{:T(128)}, f32[16]{0:T(128)S(1)}, /*index=5*/f32[16]{0:T(128)S(1)}, f32[16...) while((s32[]{:T(128)}, f32[]{:T(128)}, ...), condition=%wide.region_7.8_spmd.clone, body=%wide.region_6.7_spmd.clone.sunk | while | flops 655374 | bytes 1573133 | solution.py:28
  292.0 1.3 select_select_fusion.5
  297.8 1.3 select_select_fusion.5
  303.5 1.3 select_select_fusion.5
  309.3 1.3 select_select_fusion.5
  315.0 1.3 select_select_fusion.5
  320.8 1.3 select_select_fusion.5
  326.5 1.3 select_select_fusion.5
  332.3 1.3 select_select_fusion.5
  338.0 1.3 select_select_fusion.5
  343.8 1.3 select_select_fusion.5
  349.5 1.3 select_select_fusion.5
  355.3 1.3 select_select_fusion.5
  361.0 1.3 select_select_fusion.5
  366.8 1.3 select_select_fusion.5
  372.5 1.3 select_select_fusion.5
  378.3 1.3 select_select_fusion.5
  380.2 2.9 fusion.6
  384.6 2.2 add_convert_fusion
  386.8 3.9 copy.53
  390.8 11.3 %fusion = bf16[1024,8,128]{0,2,1:T(8,128)(2,1)} fusion(f32[8,128,1024]{2,1,0:T(8,128)} %fusion.6, bf16[1024,8,128]{0,2,1:T(8,128)(2,1)} %bitcast.105, bf16[8,1024,1024]{2,1,0:T(8,128)(2,1)} %select_convert_fusion, pred[1024]{0:T(1024)(128)(4,1)S(1)} %get-tuple-element.402), kind=kOutput, calls=%fused_computation.7 | convolution fusion | flops 2150629376 | bytes 25166848 | tf_op jit(solution)/shard_map/hts,thd->shd/dot_general | solution.py:119
  402.1 3.9 copy.52
  (112 shorter events, 61.5 us)
Async XLA Ops:
  7.2 10.5 %copy-start = (bf16[1024,1024]{1,0:T(8,128)(2,1)S(1)}, bf16[1024,1024]{1,0:T(8,128)(2,1)}, u32[]{:S(2)}) copy-start(bf16[1024,1024]{1,0:T(8,128)(2,1)} %param.12) | copy-start | bytes 6291460
  7.2 91.6 %all-gather.5.cloned.1.call-start = ((), (), s32[]{:S(2)}) async-start(), calls=%async_computation | async-start | bytes 8912896 | tf_op jit(solution)/shard_map/all_gather | solution.py:15
  12.2 4.1 copy-start.8
  17.6 4.5 %copy-start.10 = (u32[32]{0:T(128)S(1)}, u32[32]{0:T(128)}, u32[]{:S(2)}) copy-start(u32[32]{0:T(128)} %constant.101) | copy-start | bytes 388
  20.8 267.4 %all-gather.7.cloned.1.call-start = ((), (), s32[]{:S(2)}) async-start(), calls=%async_computation.1 | async-start | bytes 8912896 | tf_op jit(solution)/shard_map/all_gather | solution.py:15
  68.5 10.9 %copy-start.7 = (pred[1024,1024]{1,0:T(8,128)(4,1)}, pred[1024,1024]{1,0:T(8,128)(4,1)S(1)}, u32[]{:S(2)}) copy-start(pred[1024,1024]{1,0:T(8,128)(4,1)S(1)} %fusion.3) | copy-start | bytes 3145732
  98.8 94.4 %copy-start.9 = (f32[8]{0:T(128)S(1)}, f32[8]{0:T(128)}, u32[]{:S(2)}) copy-start(f32[8]{0:T(128)} %param.15) | copy-start | bytes 100
  205.7 7.7 %copy-start.1 = (bf16[1024,1024]{0,1:T(8,128)(2,1)S(1)}, bf16[1024,1024]{0,1:T(8,128)(2,1)}, u32[]{:S(2)}) copy-start(bf16[1024,1024]{0,1:T(8,128)(2,1)} %copy.59) | copy-start | bytes 6291460
  212.1 1.4 copy-start.2
  215.0 10.6 %copy-start.5 = (bf16[1024,8,128]{0,2,1:T(8,128)(2,1)S(1)}, bf16[1024,8,128]{0,2,1:T(8,128)(2,1)}, u32[]{:S(2)}) copy-start(bf16[1024,8,128]{0,2,1:T(8,128)(2,1)} %copy.35) | copy-start | bytes 6291460
  225.5 9.4 %copy-start.3 = (bf16[1024,8,128]{0,2,1:T(8,128)(2,1)S(1)}, bf16[1024,8,128]{0,2,1:T(8,128)(2,1)}, u32[]{:S(2)}) copy-start(bf16[1024,8,128]{0,2,1:T(8,128)(2,1)} %copy-done.2) | copy-start | bytes 6291460
  380.2 3.4 copy-start.4
  380.2 4.4 %copy-start.6 = (bf16[1024,1024]{1,0:T(8,128)(2,1)S(1)}, bf16[1024,1024]{1,0:T(8,128)(2,1)}, u32[]{:S(2)}) copy-start(bf16[1024,1024]{1,0:T(8,128)(2,1)} %param.11) | copy-start | bytes 6291460
Sparse Core Ops, SparseCore 0:
  20.9 77.8 all-gather.4
  215.1 73.1 all-gather.6
where the time goes:
time: 417 us; the launch traced here: 413 us
  loops' own time  106 us (25%)
  matrix products  84.3 us (20%)
  local copies, waits for them, and re-layouts  77 us (18%)
  other arithmetic  49.6 us (12%)
  blocking collectives  40.5 us (10%)
  waiting for transfers between devices  40 us (10%)
  between operations  15.5 us (4%)
    another operation x2, loops' own time, entering(): return lax.fori_loop(0, size, turn, start)  106 us
    select_n x32, other arithmetic, turn(): return jax.tree.map(lambda a, b: jnp.where(reached, a, b), new, before)  41.3 us
    all_gather x2, waiting for transfers between devices, entering(): everything = jax.tree.map(lambda part: lax.all_gather(part, axis), value)  40 us
    dynamic_slice x64, local copies, waits for them, and re-layouts, turn(): new = combine(before, jax.tree.map(lambda part: part[at], everything))  39.1 us
    unnamed x1, blocking collectives  35.5 us
    unnamed x32, local copies, waits for them, and re-layouts  24.3 us
    dot_general x1, matrix products, per_device(): jnp.einsum('hts,the->she', probs, inner, preferred_element_type=jnp.float32)  11.8 us
    dot_general x1, matrix products, per_device(): jnp.einsum('hts,thd->shd', dprobs, query_rows, preferred_element_type=jnp...  11.3 us
  transfers between devices with their start and end apart: 2, of which 2 were waited for; matrix products, arithmetic and copies ran while one was open for 18% of the time, Pallas kernels for 0%

commit v1 on v0

v1 whole, which is shorter than its diff:
```python
import functools

import jax
import jax.numpy as jnp
from jax import lax
from jax.experimental import pallas as pl
from jax.experimental.pallas import tpu as pltpu
from jax.sharding import PartitionSpec as P

HS = 128
EPS = 1e-05
CHUNK = 256
BF = jnp.bfloat16
F32 = jnp.float32


def dot(a, b, da, db):
    return lax.dot_general(a, b, (((da,), (db,)), ((), ())), preferred_element_type=F32)


def kernel(
    heads, blocks, head_devs, reach,
    q_hbm, k_hbm, v_hbm, g_hbm, seg_ref, gain_ref,
    att_hbm, gq_hbm, gk_hbm, gv_hbm,
    q, k, v, g, att, gq, gk, gv,
    scaled, inner, gkl, gvl, probs, masks, segc,
    use_f, use_b, in_chunk_close, in_chunk_open, in_open, in_close,
    rr, xc, accp, accx, states, ustates, state_in, state_grad,
    tail_f, got_f, comb_f, far_f, back_f, home_f,
    tail_b, got_b, comb_b, far_b, back_b, home_b,
    pc_send, pc_recv,
    load_sem, store_sem, pair_send, pair_recv, far_send, far_recv, pc_ssem, pc_rsem,
):
    rows = q.shape[0]
    chunks = rows // CHUNK
    half = heads // 2
    hr = half * HS
    pairs = blocks // 2
    me = lax.axis_index("ctx")
    hd = lax.axis_index("head")
    pair = me // 2
    core = me % 2
    partner = pair * 2 + 1 - core

    loads = [
        pltpu.make_async_copy(s, d, load_sem.at[i])
        for i, (s, d) in enumerate(((k_hbm, k), (v_hbm, v), (q_hbm, q), (g_hbm, g)))
    ]
    for cp in loads:
        cp.start()

    barrier = pltpu.get_barrier_semaphore()
    pl.semaphore_signal(barrier, inc=1, device_id={"ctx": partner}, device_id_type=pl.DeviceIdType.MESH)
    count = jnp.int32(1)
    for r in range(1, reach + 1):
        for sign in (1, -1):
            other = pair + sign * r
            ok = (other >= 0) & (other < pairs)
            count = count + ok.astype(jnp.int32)

            @pl.when(ok)
            def _(other=other):
                pl.semaphore_signal(
                    barrier, inc=1, device_id={"ctx": other * 2 + core}, device_id_type=pl.DeviceIdType.MESH
                )
    for d in range(1, head_devs):
        pl.semaphore_signal(
            barrier, inc=1, device_id={"head": (hd + d) % head_devs}, device_id_type=pl.DeviceIdType.MESH
        )
        count = count + 1

    seg_row = seg_ref[...].astype(F32)
    segc[...] = jnp.broadcast_to(seg_row, (HS, rows)).T
    opens = [segc[pl.ds(j * CHUNK, 1), :] for j in range(chunks)]
    closes = [segc[pl.ds(j * CHUNK + CHUNK - 1, 1), :] for j in range(chunks)]
    own_open, own_close = opens[0], closes[-1]

    def same(a, b):
        return jnp.where(a == b, 1.0, 0.0)

    causal = lax.broadcasted_iota(jnp.int32, (CHUNK, CHUNK), 0) >= lax.broadcasted_iota(
        jnp.int32, (CHUNK, CHUNK), 1
    )
    for j in range(chunks):
        at = pl.ds(j * CHUNK, CHUNK)
        s = segc[at, :]
        in_chunk_close[at, :] = same(s, closes[j]).astype(BF)
        in_chunk_open[at, :] = same(s, opens[j]).astype(BF)
        in_open[at, :] = same(s, own_open).astype(BF)
        in_close[at, :] = same(s, own_close).astype(BF)
        use_f[at, :] = same(s, closes[max(j - 1, 0)]).astype(BF)
        use_b[at, :] = same(s, opens[min(j + 1, chunks - 1)]).astype(BF)
        wide = jnp.concatenate([s] * (CHUNK // HS), axis=1)
        row = seg_ref[:, j * CHUNK : (j + 1) * CHUNK].astype(F32)
        masks[j] = jnp.where(causal & (wide == row), 1.0, 0.0)
    pass_f = [None] + [same(closes[j], closes[j - 1]) for j in range(1, chunks)]
    pass_b = [same(opens[j], opens[j + 1]) for j in range(chunks - 1)] + [None]

    line = lax.broadcasted_iota(jnp.int32, (8, HS), 0)
    marks = jnp.where(line == 0, own_open, own_close)
    for share in range(2):
        tail_f[share, pl.ds(hr, 8), :] = marks
        tail_b[share, pl.ds(hr, 8), :] = marks

    def cols(h):
        return pl.ds(pl.multiple_of(h * HS, HS), HS)

    def each_head(start, stop, body):
        def turn(h, _):
            body(h, cols(h))
            return 0

        lax.fori_loop(start, stop, turn, 0)

    class Exchange:
        def __init__(self, way, tail, got, comb, far, back, home, result):
            self.way, self.base = way, 0 if way > 0 else 1
            self.tail, self.got, self.comb, self.far = tail, got, comb, far
            self.back, self.home, self.result = back, home, result
            self.first = core == (0 if way > 0 else 1)
            i = self.base * 2
            self.out = pltpu.make_async_remote_copy(
                src_ref=tail.at[1 - core], dst_ref=got,
                send_sem=pair_send.at[i], recv_sem=pair_recv.at[i],
                device_id={"ctx": partner}, device_id_type=pl.DeviceIdType.MESH,
            )
            self.ret = pltpu.make_async_remote_copy(
                src_ref=back, dst_ref=home,
                send_sem=pair_send.at[i + 1], recv_sem=pair_recv.at[i + 1],
                device_id={"ctx": partner}, device_id_type=pl.DeviceIdType.MESH,
            )

        def hop(self, r):
            i = self.base * reach + r - 1
            return pltpu.make_async_remote_copy(
                src_ref=self.comb, dst_ref=self.far.at[r - 1],
                send_sem=far_send.at[i], recv_sem=far_recv.at[i],
                device_id={"ctx": (pair + self.way * r) * 2 + core},
                device_id_type=pl.DeviceIdType.MESH,
            )

        def inside(self, r):
            other = pair + r
            return (other >= 0) & (other < pairs)

        def both(self):
            other_open = self.got[pl.ds(hr, 1), :]
            other_close = self.got[pl.ds(hr + 1, 1), :]
            if self.way > 0:
                own, oth = (own_close, own_open), (other_close, other_open)
            else:
                own, oth = (own_open, own_close), (other_open, other_close)
            pick = [(jnp.where(self.first, a, b), jnp.where(self.first, b, a)) for a, b in zip(own, oth)]
            return pick

        def middle(self):
            self.out.wait()
            (tag_first, tag_last), _ = self.both()
            joined = tag_first == tag_last

            def turn(e, _):
                at = pl.ds(pl.multiple_of(e * HS, HS), HS)
                mine, other = self.tail[core, at, :], self.got[at, :]
                t_first = jnp.where(self.first, mine, other)
                t_last = jnp.where(self.first, other, mine)
                self.comb[at, :] = t_last + jnp.where(joined, t_first, 0.0)
                return 0

            lax.fori_loop(0, half, turn, 0)
            self.comb[pl.ds(hr, 8), :] = jnp.broadcast_to(tag_last, (8, HS))
            for r in range(1, reach + 1):

                @pl.when(self.inside(self.way * r))
                def _(r=r):
                    self.hop(r).start()

                @pl.when(jnp.logical_not(self.inside(-self.way * r)))
                def _(r=r):
                    self.far[r - 1] = jnp.full((hr + 8, HS), -1.0, F32)

        def near(self):
            for r in range(1, reach + 1):

                @pl.when(self.inside(-self.way * r))
                def _(r=r):
                    self.hop(r).wait_recv()

            (tag_first, _), (need_first, need_last) = self.both()
            tags = [self.far[r, pl.ds(hr, 1), :] for r in range(reach)]

            def turn(e, _):
                at = pl.ds(pl.multiple_of(e * HS, HS), HS)
                t_first = jnp.where(self.first, self.tail[core, at, :], self.got[at, :])
                x_first = jnp.zeros((HS, HS), F32)
                x_last = jnp.where(tag_first == need_last, t_first, 0.0)
                for r in range(reach):
                    c = self.far[r, at, :]
                    x_first = x_first + jnp.where(tags[r] == need_first, c, 0.0)
                    x_last = x_last + jnp.where(tags[r] == need_last, c, 0.0)
                self.back[at, :] = jnp.where(self.first, x_last, x_first)
                self.result[core * half + e] = jnp.where(self.first, x_first, x_last).astype(BF)
                return 0

            lax.fori_loop(0, half, turn, 0)
            self.ret.start()

        def finish(self):
            self.ret.wait()

            def turn(e, _):
                at = pl.ds(pl.multiple_of(e * HS, HS), HS)
                self.result[(1 - core) * half + e] = self.home[at, :].astype(BF)
                return 0

            lax.fori_loop(0, half, turn, 0)
            for r in range(1, reach + 1):

                @pl.when(self.inside(self.way * r))
                def _(r=r):
                    self.hop(r).wait_send()

    fwd = Exchange(1, tail_f, got_f, comb_f, far_f, back_f, home_f, state_in)
    bwd = Exchange(-1, tail_b, got_b, comb_b, far_b, back_b, home_b, state_grad)

    loads[0].wait()
    loads[1].wait()

    def tails(h, c):
        s = None
        for j in range(chunks):
            at = pl.ds(j * CHUNK, CHUNK)
            t = dot(k[at, c] * in_chunk_close[at, :], v[at, c], 0, 0)
            s = t if j == 0 else s * pass_f[j] + t
            if j < chunks - 1:
                states[h, j] = s.astype(BF)
        tail_f[h // half, pl.ds(pl.multiple_of((h % half) * HS, HS), HS), :] = s

    each_head(0, heads, tails)
    pl.semaphore_wait(barrier, count)
    fwd.out.start()
    loads[2].wait()

    def local(h, c):
        for j in range(chunks):
            at = pl.ds(j * CHUNK, CHUNK)
            qj = q[at, c]
            p = (dot(qj, k[at, c], 1, 1) * masks[j]).astype(BF)
            probs[h, j] = p
            o = dot(p, v[at, c], 1, 0)
            if j > 0:
                o = o + dot(qj * use_f[at, :], states[h, j - 1], 1, 0)
            scaled[at, c] = o

    early = max(1, heads // 4)
    each_head(0, early, local)
    fwd.middle()
    each_head(early, heads, local)
    loads[3].wait()
    fwd.near()
    accp[...] = jnp.zeros_like(accp)
    accx[...] = jnp.zeros_like(accx)
    fwd.finish()

    def norm(h, c):
        gain = gain_ref[h]
        for j in range(chunks):
            at = pl.ds(j * CHUNK, CHUNK)
            a = scaled[at, c] + dot(q[at, c] * in_open[at, :], state_in[h], 1, 0)
            a = a * gain
            scaled[at, c] = a
            accp[at, :] += a * a
            accx[at, :] += a * g[at, c].astype(F32)

    each_head(0, heads, norm)

    pc_send[pl.ds(0, 1), :] = jnp.sum(accp[...].T, axis=0, keepdims=True)
    pc_send[pl.ds(1, 1), :] = jnp.sum(accx[...].T, axis=0, keepdims=True)
    pc_send[pl.ds(2, 6), :] = jnp.zeros((6, rows), F32)
    swaps = [
        pltpu.make_async_remote_copy(
            src_ref=pc_send, dst_ref=pc_recv.at[d - 1],
            send_sem=pc_ssem.at[d - 1], recv_sem=pc_rsem.at[d - 1],
            device_id={"head": (hd + d) % head_devs}, device_id_type=pl.DeviceIdType.MESH,
        )
        for d in range(1, head_devs)
    ]
    for cp in swaps:
        cp.start()
    for cp in swaps:
        cp.wait()
    power, cross = pc_send[pl.ds(0, 1), :], pc_send[pl.ds(1, 1), :]
    for d in range(head_devs - 1):
        power = power + pc_recv[d, pl.ds(0, 1), :]
        cross = cross + pc_recv[d, pl.ds(1, 1), :]
    width = head_devs * heads * HS
    r = lax.rsqrt(power / width + EPS)
    rr[...] = jnp.broadcast_to(r, (HS, rows)).T
    xc[...] = jnp.broadcast_to(cross * r * r * r / width, (HS, rows)).T

    def inners(h, c):
        gain = gain_ref[h]
        u = None
        for j in reversed(range(chunks)):
            at = pl.ds(j * CHUNK, CHUNK)
            a, rj = scaled[at, c], rr[at, :]
            att[at, c] = (a * rj).astype(BF)
            i = (gain * (g[at, c].astype(F32) * rj - a * xc[at, :])).astype(BF)
            inner[at, c] = i
            b = dot(q[at, c] * in_chunk_open[at, :], i, 0, 0)
            u = b if j == chunks - 1 else u * pass_b[j] + b
            if j > 0:
                ustates[h, j - 1] = u.astype(BF)
        tail_b[h // half, pl.ds(pl.multiple_of((h % half) * HS, HS), HS), :] = u

    each_head(0, heads, inners)
    bwd.out.start()
    stores = [
        pltpu.make_async_copy(s, d, store_sem.at[i])
        for i, (s, d) in enumerate(((att, att_hbm), (gq, gq_hbm), (gk, gk_hbm), (gv, gv_hbm)))
    ]
    stores[0].start()

    def grads(h, c):
        for j in range(chunks):
            at = pl.ds(j * CHUNK, CHUNK)
            i, kj, vj = inner[at, c], k[at, c], v[at, c]
            d = (dot(i, vj, 1, 1) * masks[j]).astype(BF)
            a = dot(d, kj, 1, 0) + dot(i * in_open[at, :], state_in[h], 1, 1)
            if j > 0:
                a = a + dot(i * use_f[at, :], states[h, j - 1], 1, 1)
            gq[at, c] = a.astype(BF)
            b = dot(d, q[at, c], 0, 0)
            e = dot(probs[h, j], i, 0, 0)
            if j < chunks - 1:
                b = b + dot(vj * use_b[at, :], ustates[h, j], 1, 1)
                e = e + dot(kj * use_b[at, :], ustates[h, j], 1, 0)
            gkl[at, c] = b
            gvl[at, c] = e

    each_head(0, early, grads)
    bwd.middle()
    each_head(early, heads, grads)
    stores[1].start()
    bwd.near()
    bwd.finish()

    def last(h, c):
        for j in range(chunks):
            at = pl.ds(j * CHUNK, CHUNK)
            m = in_close[at, :]
            gk[at, c] = (gkl[at, c] + dot(v[at, c] * m, state_grad[h], 1, 1)).astype(BF)
            gv[at, c] = (gvl[at, c] + dot(k[at, c] * m, state_grad[h], 1, 0)).astype(BF)

    each_head(0, heads, last)
    stores[2].start()
    stores[3].start()
    for cp in stores:
        cp.wait()


def per_device(queries, key_vectors, value_vectors, out_grad, segment_ids, head_gain):
    rows, width = queries.shape
    heads = head_gain.shape[0]
    blocks = lax.axis_size("ctx")
    head_devs = lax.axis_size("head")
    reach = max(1, (blocks // 4 + 1) // 2)
    chunks = rows // CHUNK
    hr = heads // 2 * HS
    V = pltpu.VMEM
    whole = V((rows, width), BF)
    lanes = V((rows, HS), BF)
    flanes = V((rows, HS), F32)
    msg = V((hr + 8, HS), F32)
    comm = [V((2, hr + 8, HS), F32), msg, msg, V((reach, hr + 8, HS), F32), V((hr, HS), F32), V((hr, HS), F32)]
    peers = max(1, head_devs - 1)
    dma = pltpu.SemaphoreType.DMA
    scratch = (
        [whole] * 8
        + [V((rows, width), F32), whole, V((rows, width), F32), V((rows, width), F32)]
        + [V((heads, chunks, CHUNK, CHUNK), BF), V((chunks, CHUNK, CHUNK), F32), flanes]
        + [lanes] * 6
        + [flanes] * 4
        + [V((heads, chunks - 1, HS, HS), BF)] * 2
        + [V((heads, HS, HS), BF)] * 2
        + comm
        + comm
        + [V((8, rows), F32), V((peers, 8, rows), F32)]
        + [dma((4,)), dma((4,)), dma((4,)), dma((4,)), dma((2 * reach,)), dma((2 * reach,)), dma((peers,)), dma((peers,))]
    )
    out = jax.ShapeDtypeStruct((rows, width), BF)
    anywhere = pl.BlockSpec(memory_space=pl.ANY)
    return pl.pallas_call(
        functools.partial(kernel, heads, blocks, head_devs, reach),
        out_shape=[out] * 4,
        in_specs=[anywhere] * 4
        + [pl.BlockSpec(memory_space=pltpu.VMEM), pl.BlockSpec(memory_space=pltpu.SMEM)],
        out_specs=[anywhere] * 4,
        scratch_shapes=scratch,
        compiler_params=pltpu.CompilerParams(
            collective_id=0, has_side_effects=True, vmem_limit_bytes=56 * 1024 * 1024
        ),
    )(queries, key_vectors, value_vectors, out_grad, segment_ids.reshape(1, rows), head_gain)


def solution(mesh):
    wide = P("ctx", "head")
    return jax.shard_map(
        per_device,
        mesh=mesh,
        in_specs=(wide, wide, wide, wide, P("ctx"), P("head")),
        out_specs=(wide, wide, wide, wide),
        check_vma=False,
    )
```

time: 417 us -> 61.7 us (0.15)
  loops' own time: 106 us -> 0 us
  matrix products: 84.3 us -> 0 us
  local copies, waits for them, and re-layouts: 77 us -> 9.25 us
  Pallas kernels: 0 us -> 51.5 us
  other arithmetic: 49.6 us -> 0 us
  blocking collectives: 40.5 us -> 0 us
  waiting for transfers between devices: 40 us -> 0 us
  between operations: 15.5 us -> 0.65 us
    another operation x2 -> x0, loops' own time: 106 us -> none  [entering(): return lax.fori_loop(0, size, turn, start)]
    dot_general x12 -> x0, matrix products: 84.3 us -> none  [the longest x1 11.8 us: per_device(): jnp.einsum('hts,the->she', probs, inner, preferred_element_type=jnp.float32)]
    pallas_call x0 -> x1, Pallas kernels: none -> 51.5 us  [per_device(): pl.pallas_call(functools.partial(kernel, heads, blocks, head_devs, reach)...]
    select_n x32 -> x0, other arithmetic: 41.3 us -> none  [turn(): return jax.tree.map(lambda a, b: jnp.where(reached, a, b), new, before)]
    all_gather x2 -> x0, waiting for transfers between devices: 40 us -> none  [entering(): everything = jax.tree.map(lambda part: lax.all_gather(part, axis), value)]
    dynamic_slice x64 -> x0, local copies, waits for them, and re-layouts: 39.1 us -> none  [turn(): new = combine(before, jax.tree.map(lambda part: part[at], everything))]
    unnamed x1 -> x0, blocking collectives: 35.5 us -> none
    unnamed x32 -> x10, local copies, waits for them, and re-layouts: 24.3 us -> 9.25 us
  transfers between devices with their start and end apart: 2 -> 0, of which waited for: 2 -> 0; matrix products, arithmetic and copies ran while one was open for 18% -> 0% of each run, Pallas kernels for 0% -> 0%
where the time goes in v1:
time: 61.7 us; the launch traced here: 61.4 us
  Pallas kernels  51.5 us (83%)
  local copies, waits for them, and re-layouts  9.25 us (15%)
  between operations  0.65 us (1%)
    pallas_call x1, Pallas kernels, per_device(): pl.pallas_call(functools.partial(kernel, heads, blocks, head_devs, reach)...  51.5 us
    unnamed x10, local copies, waits for them, and re-layouts  9.25 us

profile of v1, /device:TPU:0, one launch (start us, length us, event | category | flops | bytes accessed | tf_op | source)
XLA Modules:
  0.0 61.4 jit_solution(6814891431194428356)
XLA Ops:
  0.6 51.5 %shard_map.93 = (bf16[1024,1024]{1,0:T(8,128)(2,1)}, bf16[1024,1024]{1,0:T(8,128)(2,1)}, bf16[1024,1024]{1,0:T(8,128)(2,1)}, bf16[1024,1024]{1,0:T(8,128)(2,1)}) custom-call(bf16[1024,1024]{1,0:T(8,128)(2,1)} %q_hbm.1, bf16[1024,1024]{1,0:T(8,128)(2,1)} %k_hbm.1, bf16[1024,1024]{1,0:T(8,128)(2,1)} %v_hbm.1, bf16[1024,1024]{1,0:T(8,128)(2,1)} %g_hbm.1, ...), custom_call_target="tpu_custom_call" | custom-call | tf_op jit(solution)/shard_map/pallas_call | solution.py:392
  52.2 0.0 copy-start.2
  52.2 3.2 %copy.14 = bf16[1024,1024]{1,0:T(8,128)(2,1)} copy(bf16[1024,1024]{1,0:T(8,128)(2,1)} %get-tuple-element.8) | data formatting | bytes 4194304
  55.4 0.0 copy-done.2
  55.4 0.0 copy-start.1
  55.4 1.3 %copy.15 = bf16[1024,1024]{1,0:T(8,128)(2,1)} copy(bf16[1024,1024]{1,0:T(8,128)(2,1)S(1)} %copy-done.2) | data formatting | bytes 4194304
  56.7 1.0 %copy-done.1 = bf16[1024,1024]{1,0:T(8,128)(2,1)S(1)} copy-done((bf16[1024,1024]{1,0:T(8,128)(2,1)S(1)}, bf16[1024,1024]{1,0:T(8,128)(2,1)}, u32[]{:S(2)}) %copy-start.1) | copy-done | bytes 2097176
  57.8 0.0 copy-start
  57.8 1.3 %copy.16 = bf16[1024,1024]{1,0:T(8,128)(2,1)} copy(bf16[1024,1024]{1,0:T(8,128)(2,1)S(1)} %copy-done.1) | data formatting | bytes 4194304
  59.1 1.0 %copy-done = bf16[1024,1024]{1,0:T(8,128)(2,1)S(1)} copy-done((bf16[1024,1024]{1,0:T(8,128)(2,1)S(1)}, bf16[1024,1024]{1,0:T(8,128)(2,1)}, u32[]{:S(2)}) %copy-start) | copy-done | bytes 2097176
  60.1 1.3 %copy.17 = bf16[1024,1024]{1,0:T(8,128)(2,1)} copy(bf16[1024,1024]{1,0:T(8,128)(2,1)S(1)} %copy-done) | data formatting | bytes 4194304
Async XLA Ops:
  52.2 3.2 %copy-start.2 = (bf16[1024,1024]{1,0:T(8,128)(2,1)S(1)}, bf16[1024,1024]{1,0:T(8,128)(2,1)}, u32[]{:S(2)}) copy-start(bf16[1024,1024]{1,0:T(8,128)(2,1)} %get-tuple-element.9) | copy-start | bytes 6291460
  55.4 2.3 %copy-start.1 = (bf16[1024,1024]{1,0:T(8,128)(2,1)S(1)}, bf16[1024,1024]{1,0:T(8,128)(2,1)}, u32[]{:S(2)}) copy-start(bf16[1024,1024]{1,0:T(8,128)(2,1)} %get-tuple-element.10) | copy-start | bytes 6291460
  57.8 2.3 %copy-start = (bf16[1024,1024]{1,0:T(8,128)(2,1)S(1)}, bf16[1024,1024]{1,0:T(8,128)(2,1)}, u32[]{:S(2)}) copy-start(bf16[1024,1024]{1,0:T(8,128)(2,1)} %get-tuple-element.11) | copy-start | bytes 6291460

commit v2 on v1

--- a/solution.py
+++ b/solution.py
@@ -21,15 +21,15 @@
 def kernel(
     heads, blocks, head_devs, reach,
     q_hbm, k_hbm, v_hbm, g_hbm, seg_ref, gain_ref,
-    att_hbm, gq_hbm, gk_hbm, gv_hbm,
-    q, k, v, g, att, gq, gk, gv,
+    att_hbm, gq_hbm, gkl_hbm, gvl_hbm, close_out, grad_out,
+    q, k, v, g, att, gq,
     scaled, inner, gkl, gvl, probs, masks, segc,
     use_f, use_b, in_chunk_close, in_chunk_open, in_open, in_close,
     rr, xc, accp, accx, states, ustates, state_in, state_grad,
     tail_f, got_f, comb_f, far_f, back_f, home_f,
     tail_b, got_b, comb_b, far_b, back_b, home_b,
     pc_send, pc_recv,
-    load_sem, store_sem, pair_send, pair_recv, far_send, far_recv, pc_ssem, pc_rsem,
+    load_sem, kv_sem, store_sem, part_sem, pair_send, pair_recv, far_send, far_recv, pc_ssem, pc_rsem,
 ):
     rows = q.shape[0]
     chunks = rows // CHUNK
@@ -44,8 +44,24 @@
 
     loads = [
         pltpu.make_async_copy(s, d, load_sem.at[i])
-        for i, (s, d) in enumerate(((k_hbm, k), (v_hbm, v), (q_hbm, q), (g_hbm, g)))
+        for i, (s, d) in enumerate(((q_hbm, q), (g_hbm, g)))
     ]
+
+    def cols(h):
+        return pl.ds(pl.multiple_of(h * HS, HS), HS)
+
+    def kv_load(h):
+        return [
+            pltpu.make_async_copy(s.at[:, cols(h)], d.at[:, cols(h)], kv_sem.at[i, h])
+            for i, (s, d) in enumerate(((k_hbm, k), (v_hbm, v)))
+        ]
+
+    def start_kv(h, _):
+        for cp in kv_load(h):
+            cp.start()
+        return 0
+
+    lax.fori_loop(0, heads, start_kv, 0)
     for cp in loads:
         cp.start()
 
@@ -102,15 +118,12 @@
         tail_f[share, pl.ds(hr, 8), :] = marks
         tail_b[share, pl.ds(hr, 8), :] = marks
 
-    def cols(h):
-        return pl.ds(pl.multiple_of(h * HS, HS), HS)
-
     def each_head(start, stop, body):
         def turn(h, _):
             body(h, cols(h))
             return 0
 
-        lax.fori_loop(start, stop, turn, 0)
+        lax.fori_loop(start, stop, turn, 0, unroll=2 if (stop - start) % 2 == 0 else 1)
 
     class Exchange:
         def __init__(self, way, tail, got, comb, far, back, home, result):
@@ -222,10 +235,9 @@
     fwd = Exchange(1, tail_f, got_f, comb_f, far_f, back_f, home_f, state_in)
     bwd = Exchange(-1, tail_b, got_b, comb_b, far_b, back_b, home_b, state_grad)
 
-    loads[0].wait()
-    loads[1].wait()
-
     def tails(h, c):
+        for cp in kv_load(h):
+            cp.wait()
         s = None
         for j in range(chunks):
             at = pl.ds(j * CHUNK, CHUNK)
@@ -238,7 +250,7 @@
     each_head(0, heads, tails)
     pl.semaphore_wait(barrier, count)
     fwd.out.start()
-    loads[2].wait()
+    loads[0].wait()
 
     def local(h, c):
         for j in range(chunks):
@@ -255,7 +267,7 @@
     each_head(0, early, local)
     fwd.middle()
     each_head(early, heads, local)
-    loads[3].wait()
+    loads[1].wait()
     fwd.near()
     accp[...] = jnp.zeros_like(accp)
     accx[...] = jnp.zeros_like(accx)
@@ -316,9 +328,15 @@
     bwd.out.start()
     stores = [
         pltpu.make_async_copy(s, d, store_sem.at[i])
-        for i, (s, d) in enumerate(((att, att_hbm), (gq, gq_hbm), (gk, gk_hbm), (gv, gv_hbm)))
+        for i, (s, d) in enumerate(((att, att_hbm), (gq, gq_hbm)))
     ]
     stores[0].start()
+
+    def parts(h):
+        return [
+            pltpu.make_async_copy(s.at[:, cols(h)], d.at[:, cols(h)], part_sem.at[i, h])
+            for i, (s, d) in enumerate(((gkl, gkl_hbm), (gvl, gvl_hbm)))
+        ]
 
     def grads(h, c):
         for j in range(chunks):
@@ -336,6 +354,8 @@
                 e = e + dot(kj * use_b[at, :], ustates[h, j], 1, 0)
             gkl[at, c] = b
             gvl[at, c] = e
+        for cp in parts(h):
+            cp.start()
 
     each_head(0, early, grads)
     bwd.middle()
@@ -344,18 +364,27 @@
     bwd.near()
     bwd.finish()
 
-    def last(h, c):
-        for j in range(chunks):
-            at = pl.ds(j * CHUNK, CHUNK)
-            m = in_close[at, :]
-            gk[at, c] = (gkl[at, c] + dot(v[at, c] * m, state_grad[h], 1, 1)).astype(BF)
-            gv[at, c] = (gvl[at, c] + dot(k[at, c] * m, state_grad[h], 1, 0)).astype(BF)
-
-    each_head(0, heads, last)
-    stores[2].start()
-    stores[3].start()
+    close_out[...] = in_close[...]
+    grad_out[...] = state_grad[...]
+
+    def drain(h, _):
+        for cp in parts(h):
+            cp.wait()
+        return 0
+
+    lax.fori_loop(0, heads, drain, 0)
     for cp in stores:
         cp.wait()
+
+
+def finish_kernel(heads, att, gq, gkl, gvl, k, v, close, grad, att_out, gq_out, gk_out, gv_out):
+    att_out[...] = att[...]
+    gq_out[...] = gq[...]
+    m = close[...]
+    for h in range(heads):
+        c = slice(h * HS, (h + 1) * HS)
+        gk_out[:, c] = (gkl[:, c] + dot(v[:, c] * m, grad[h], 1, 1)).astype(BF)
+        gv_out[:, c] = (gvl[:, c] + dot(k[:, c] * m, grad[h], 1, 0)).astype(BF)
 
 
 def per_device(queries, key_vectors, value_vectors, out_grad, segment_ids, head_gain):
@@ -375,7 +404,7 @@
     peers = max(1, head_devs - 1)
     dma = pltpu.SemaphoreType.DMA
     scratch = (
-        [whole] * 8
+        [whole] * 6
         + [V((rows, width), F32), whole, V((rows, width), F32), V((rows, width), F32)]
         + [V((heads, chunks, CHUNK, CHUNK), BF), V((chunks, CHUNK, CHUNK), F32), flanes]
         + [lanes] * 6
@@ -385,21 +414,33 @@
         + comm
         + comm
         + [V((8, rows), F32), V((peers, 8, rows), F32)]
-        + [dma((4,)), dma((4,)), dma((4,)), dma((4,)), dma((2 * reach,)), dma((2 * reach,)), dma((peers,)), dma((peers,))]
+        + [dma((2,)), dma((2, heads)), dma((2,)), dma((2, heads)), dma((4,)), dma((4,)), dma((2 * reach,)), dma((2 * reach,)), dma((peers,)), dma((peers,))]
     )
     out = jax.ShapeDtypeStruct((rows, width), BF)
     anywhere = pl.BlockSpec(memory_space=pl.ANY)
-    return pl.pallas_call(
+    part = jax.ShapeDtypeStruct((rows, width), F32)
+    att, gq, gkl, gvl, close, grad = pl.pallas_call(
         functools.partial(kernel, heads, blocks, head_devs, reach),
-        out_shape=[out] * 4,
+        out_shape=[out, out, part, part, jax.ShapeDtypeStruct((rows, HS), BF), jax.ShapeDtypeStruct((heads, HS, HS), BF)],
         in_specs=[anywhere] * 4
         + [pl.BlockSpec(memory_space=pltpu.VMEM), pl.BlockSpec(memory_space=pltpu.SMEM)],
-        out_specs=[anywhere] * 4,
+        out_specs=[anywhere] * 4 + [pl.BlockSpec(memory_space=pltpu.VMEM)] * 2,
         scratch_shapes=scratch,
         compiler_params=pltpu.CompilerParams(
             collective_id=0, has_side_effects=True, vmem_limit_bytes=56 * 1024 * 1024
         ),
     )(queries, key_vectors, value_vectors, out_grad, segment_ids.reshape(1, rows), head_gain)
+    step = 128
+    wide = pl.BlockSpec((step, width), lambda i: (i, 0))
+    return pl.pallas_call(
+        functools.partial(finish_kernel, heads),
+        grid=(rows // step,),
+        out_shape=[out] * 4,
+        in_specs=[wide] * 6
+        + [pl.BlockSpec((step, HS), lambda i: (i, 0)), pl.BlockSpec((heads, HS, HS), lambda i: (0, 0, 0))],
+        out_specs=[wide] * 4,
+        compiler_params=pltpu.CompilerParams(vmem_limit_bytes=56 * 1024 * 1024),
+    )(att, gq, gkl, gvl, key_vectors, value_vectors, close, grad)
 
 
 def solution(mesh):

time: 61.7 us -> 58.5 us (0.948)
  local copies, waits for them, and re-layouts: 9.25 us -> 0 us
  Pallas kernels: 51.5 us -> 57.6 us
    pallas_call x0 -> x1, Pallas kernels: none -> 11.8 us  [per_device(): pl.pallas_call(functools.partial(finish_kernel, heads), grid=(rows // ste...]
    unnamed x10 -> x0, local copies, waits for them, and re-layouts: 9.25 us -> none
    pallas_call x1, Pallas kernels: 51.5 us -> 45.8 us  [per_device(): pl.pallas_call(functools.partial(kernel, heads, blocks, head_devs, reach)...]
where the time goes in v2:
time: 58.5 us; the launch traced here: 58.2 us
  Pallas kernels  57.6 us (98%)
  between operations  0.64 us (1%)
    pallas_call x1, Pallas kernels, per_device(): pl.pallas_call(functools.partial(kernel, heads, blocks, head_devs, reach)...  45.8 us
    pallas_call x1, Pallas kernels, per_device(): pl.pallas_call(functools.partial(finish_kernel, heads), grid=(rows // ste...  11.8 us

profile of v2, /device:TPU:0, one launch (start us, length us, event | category | flops | bytes accessed | tf_op | source)
XLA Modules:
  0.0 58.2 jit_solution(6296099289456185614)
XLA Ops:
  0.6 45.8 %shard_map.93 = (bf16[1024,1024]{1,0:T(8,128)(2,1)}, bf16[1024,1024]{1,0:T(8,128)(2,1)}, f32[1024,1024]{1,0:T(8,128)}, f32[1024,1024]{1,0:T(8,128)}, bf16[1024,1...) custom-call(bf16[1024,1024]{1,0:T(8,128)(2,1)} %q_hbm.1, bf16[1024,1024]{1,0:T(8,128)(2,1)} %k.1, bf16[1024,1024]{1,0:T(8,128)(2,1)} %v.1, ...), custom_call_target="tpu_custom_call" | custom-call | tf_op jit(solution)/shard_map/pallas_call | solution.py:422
  46.4 11.8 %shard_map.94 = (bf16[1024,1024]{1,0:T(8,128)(2,1)}, bf16[1024,1024]{1,0:T(8,128)(2,1)}, bf16[1024,1024]{1,0:T(8,128)(2,1)}, bf16[1024,1024]{1,0:T(8,128)(2,1)}) custom-call(bf16[1024,1024]{1,0:T(8,128)(2,1)} %get-tuple-element.10.att, bf16[1024,1024]{1,0:T(8,128)(2,1)} %get-tuple-element.11.gq, f32[1024,1024]{1,0:T(8,128)} %get-tuple-element.12.gkl, ...), custom_call_target="tpu_custom_call" | custom-call | tf_op jit(solution)/shard_map/pallas_call | solution.py:435
